TPU v7x, 256 devices: a whole 4x4x8 slice. The times are simulated.
256 devices in a mesh: dp: 16 (over y, x_hi, core), mp: 16 (over x_lo, z).
Axes of the slice: x: 4 (x_hi: 2, x_lo: 2; x = x_hi * 2 + x_lo), y: 4, z: 8, core: 2. Of those that a mesh axis runs over, the one named last changes fastest.
Arguments:
- activations: bfloat16 [16384, 4096], P('dp', 'mp'), may hold values from -6 to 6
- out_grads: bfloat16 [16384, 512], P(('dp', 'mp')), may hold values from -6 to 6
- doc_slot: int32 [16384], P('dp'), may hold values from 0 to 7
- input_eigenvectors: bfloat16 [4096, 4096], P(None, 'mp'), as said below
- eigen_out: bfloat16 [512, 512], replicated, as said below
- query_tiles: bfloat16 [32, 512, 4096], P(None, 'dp', 'mp'), may hold values from -6 to 6
- query_pick: int32 [16], replicated, may hold values from 0 to 31, as said below
Outputs:
- preconditioned: bfloat16 [4096, 16, 512], P('mp', None, 'dp')
Inputs may be any that keep to these rules, and one draw needn't show every extreme that they name: `doc_slot`: numbers name documents within the row's own group. `query_pick`: 16 different indices, among them 0 and 31, in no particular order. `input_eigenvectors`: Real-valued basis matrix with columns of unequal length. `eigen_out`: Real-valued basis matrix with columns of unequal length.
All inputs are finite; a program needn't handle non-finite values.
Results may differ from a plain program's by a relative error of at most 0.011.
Values may be sent and summed in bfloat16 or wider, within the bound.
A program may use at most 64 MiB of HBM per device.

v0:
```python
import jax
import jax.numpy as jnp
from jax import lax
from jax.sharding import PartitionSpec as P

DOC_G = 8


DAMPING = 0.1


def shards(
    activations, out_grads, doc_slot, input_eigenvectors, eigen_out, query_tiles, query_pick
):
    local_cols = input_eigenvectors.shape[1]
    basis_part = input_eigenvectors
    rotated_in = jnp.dot(
        lax.all_gather(activations, "mp", axis=1, tiled=True),
        basis_part,
        preferred_element_type=jnp.float32,
    ).astype(jnp.bfloat16)
    rotated_out = jnp.dot(
        lax.all_gather(out_grads, "mp", axis=0, tiled=True),
        eigen_out,
        preferred_element_type=jnp.float32,
    ).astype(jnp.bfloat16)
    onehot = (doc_slot[None, :] == jnp.arange(DOC_G, dtype=jnp.int32)[:, None]).astype(jnp.bfloat16)
    masked_entries = onehot[:, :, None] * rotated_out[None]
    doc_grad = jnp.einsum(
        "nre,rk->nek", masked_entries, rotated_in, preferred_element_type=jnp.float32
    )
    partial_sq = jnp.sum(doc_grad * doc_grad, axis=0)
    owner_rows = query_tiles.shape[1]
    summed = lax.psum(partial_sq, "dp")
    owned = lax.dynamic_slice_in_dim(summed, lax.axis_index("dp") * owner_rows, owner_rows, 0)
    eigen_vals = owned / (DOC_G * lax.axis_size("dp"))
    chosen = jnp.take(query_tiles, query_pick, axis=0).astype(jnp.float32)
    rescaled_gradient = (chosen / (eigen_vals[None] + DAMPING)).astype(jnp.bfloat16)
    selected = rescaled_gradient.shape[0]
    flat_tiles = rescaled_gradient.reshape(selected * owner_rows, local_cols)
    basis_part = input_eigenvectors
    final_output = lax.psum_scatter(
        lax.dot_general(
            basis_part, flat_tiles, (((1,), (1,)), ((), ())), preferred_element_type=jnp.float32
        ),
        "mp",
        scatter_dimension=0,
        tiled=True,
    )
    return final_output.reshape(final_output.shape[0], selected, owner_rows).astype(jnp.bfloat16)


def solution(mesh):
    in_specs = (
        P("dp", "mp"),
        P(("dp", "mp"), None),
        P("dp"),
        P(None, "mp"),
        P(),
        P(None, "dp", "mp"),
        P(),
    )
    out_specs = P("mp", None, "dp")
    return jax.shard_map(shards, mesh=mesh, in_specs=in_specs, out_specs=out_specs, check_vma=False)
```

profile of v0, /device:TPU:2, one launch (start us, length us, event | category | flops | bytes accessed | tf_op | source)
XLA Modules:
  0.0 476.3 jit_solution(12855527956758220249)
XLA Ops:
  6.5 0.0 copy-start
  6.5 0.0 all-gather.3.cloned.1.call-start
  6.5 0.7 all-gather.3.cloned.1.call-update
  7.3 0.0 all-gather.5.cloned.1.call-start
  7.3 0.7 all-gather.5.cloned.1.call-update
  8.0 0.0 all-reduce.2.cloned.1.call-start
  8.1 0.7 fusion.8
  8.8 71.6 %all-gather.3.cloned.1.call-done = bf16[1024,512]{1,0:T(8,128)(2,1)} async-done(((bf16[64,512]{1,0:T(8,128)(2,1)}), bf16[1024,512]{1,0:T(8,128)(2,1)}) %all-gather.3.cloned.1.call-update) | async-done | bytes 1048592 | tf_op jit(solution)/shard_map/all_gather | solution.py:23
  80.4 3.2 convolution_convert_fusion
  83.6 0.0 copy-start.2
  83.6 0.0 copy-start.1
  83.6 121.2 %all-gather.5.cloned.1.call-done = bf16[1024,4096]{1,0:T(8,128)(2,1)} async-done(((bf16[1024,256]{1,0:T(8,128)(2,1)}), bf16[1024,4096]{1,0:T(8,128)(2,1)}) %all-gather.5.cloned.1.call-update) | async-done | bytes 8388624 | tf_op jit(solution)/shard_map/all_gather | solution.py:18
  204.8 0.0 copy-done
  204.8 13.3 %multiply_reduce_fusion = f32[512,256]{1,0:T(8,128)} fusion(bf16[1024,512]{0,1:T(8,128)(2,1)} %convolution_convert_fusion, bf16[8,1024]{1,0:T(8,128)(2,1)S(1)} %fusion.8, bf16[1024,4096]{1,0:T(8,128)(2,1)} %all-gather.5.cloned.1.call-done, bf16[4096,256]{1,0:T(8,128)(2,1)S(1)} %copy-done), kind=kOutput, calls=%fused_computation.4 | convolution fusion | flops 4301389824 | bytes 12075008 | tf_op jit(solution)/shard_map/nre,rk->nek/dot_general | solution.py:29
  218.1 0.0 all-reduce.2.cloned.1.call-update
  218.1 0.0 reduce-scatter.2.cloned.1.call-start
  218.2 0.0 copy-done.2
  218.2 0.1 broadcast_in_dim.21
  218.3 0.1 broadcast_in_dim.22
  218.4 0.0 copy-done.1
  218.4 0.6 gather_fusion
  219.0 141.6 %all-reduce.2.cloned.1.call-done = f32[512,256]{1,0:T(8,128)} async-done(((f32[512,256]{1,0:T(8,128)}), f32[512,256]{1,0:T(8,128)}) %all-reduce.2.cloned.1.call-update) | async-done | bytes 524304 | tf_op jit(solution)/shard_map/psum | solution.py:34
  360.6 0.8 multiply_add_fusion
  361.3 0.1 fusion.7
  361.5 4.5 convolution_bitcast_fusion
  366.0 0.0 reduce-scatter.2.cloned.1.call-update
  366.0 101.9 %reduce-scatter.2.cloned.1.call-done = f32[256,512]{0,1:T(8,128)} async-done(((f32[4096,512]{0,1:T(8,128)}), f32[256,512]{0,1:T(8,128)}) %reduce-scatter.2.cloned.1.call-update) | async-done | bytes 524304 | tf_op jit(solution)/shard_map/reduce_scatter | solution.py:42
  468.0 1.8 convert_element_type.32
  (3 shorter events, 0.0 us)
Async XLA Ops:
  6.5 198.3 %copy-start = (bf16[4096,256]{1,0:T(8,128)(2,1)S(1)}, bf16[4096,256]{1,0:T(8,128)(2,1)}, u32[]{:S(2)}) copy-start(bf16[4096,256]{1,0:T(8,128)(2,1)} %param.10) | copy-start | bytes 6291460
  6.5 73.9 %all-gather.3.cloned.1.call-start = ((), (), s32[]{:S(2)}) async-start(), calls=%async_computation.1 | async-start | bytes 1114112 | tf_op jit(solution)/shard_map/all_gather | solution.py:23
  7.3 197.5 %all-gather.5.cloned.1.call-start = ((), (), s32[]{:S(2)}) async-start(), calls=%async_computation.2 | async-start | bytes 8912896 | tf_op jit(solution)/shard_map/all_gather | solution.py:18
  8.0 352.6 %all-reduce.2.cloned.1.call-start = ((), (), s32[]{:S(2)}) async-start(), calls=%async_computation.3 | async-start | bytes 1048576 | tf_op jit(solution)/shard_map/psum | solution.py:34
  83.6 134.6 %copy-start.2 = (s32[16]{0:T(128)S(1)}, s32[16]{0:T(128)}, u32[]{:S(2)}) copy-start(s32[16]{0:T(128)} %param.13) | copy-start | bytes 196
  83.6 134.8 %copy-start.1 = (bf16[32,32,256]{2,1,0:T(8,128)(2,1)S(1)}, bf16[32,32,256]{2,1,0:T(8,128)(2,1)}, u32[]{:S(2)}) copy-start(bf16[32,32,256]{2,1,0:T(8,128)(2,1)} %param.12) | copy-start | bytes 1572868
  218.1 249.8 %reduce-scatter.2.cloned.1.call-start = ((), (), s32[]{:S(2)}) async-start(), calls=%async_computation.4 | async-start | bytes 8912896 | tf_op jit(solution)/shard_map/reduce_scatter | solution.py:42
Sparse Core Ops, SparseCore 0:
  9.1 71.2 all-gather.2
  82.1 122.6 all-gather.4
  218.2 142.2 all-reduce.1
  366.1 101.7 reduce-scatter.1
where the time goes:
time: 478 us; the launch traced here: 476 us
  waiting for transfers between devices  438 us (92%)
  matrix products  21 us (4%)
  between operations  13.2 us (3%)
    psum x1, waiting for transfers between devices, shards(): summed = lax.psum(partial_sq, 'dp')  142 us
    all_gather x1, waiting for transfers between devices, shards(): lax.all_gather(activations, 'mp', axis=1, tiled=True)  121 us
    reduce_scatter x1, waiting for transfers between devices, shards(): lax.psum_scatter(lax.dot_general(basis_part, flat_tiles, (((1,), (1,)), (...  102 us
    all_gather x1, waiting for transfers between devices, shards(): lax.all_gather(out_grads, 'mp', axis=0, tiled=True)  71.6 us
    dot_general x1, matrix products, shards(): jnp.einsum('nre,rk->nek', masked_entries, rotated_in, preferred_element_t...  13.3 us
  transfers between devices with their start and end apart: 4, of which 4 were waited for; matrix products, arithmetic and copies ran while one was open for 1% of the time, Pallas kernels for 0%

commit v1 on v0

v1 whole, which is shorter than its diff:
```python
import functools

import jax
import jax.numpy as jnp
from jax import lax
from jax.experimental import pallas as pl
from jax.experimental.pallas import tpu as pltpu
from jax.sharding import PartitionSpec as P

DOC_G = 8
DAMPING = 0.1
PAIR = 2
UNITS = 4
MESH = pl.DeviceIdType.MESH
F32 = jnp.float32
BF16 = jnp.bfloat16


def fused(
    n_dp,
    n_mp,
    act,
    og,
    slots,
    vecs,
    eo,
    tiles,
    pick,
    out,
    a_buf,
    v_buf,
    og_buf,
    eo_buf,
    q_buf,
    ro_buf,
    own_buf,
    psend,
    precv,
    acc,
    sq_send,
    sq_own,
    sq_recv,
    sc,
    r_send,
    r_recv,
    load_sem,
    a_send_sem,
    a_recv_sem,
    v_send_sem,
    v_recv_sem,
    o_send_sem,
    o_recv_sem,
    ox_send_sem,
    ox_recv_sem,
    p_send_sem,
    p_recv_sem,
    sq_send_sem,
    sq_recv_sem,
    sc_sems,
    r_send_sem,
    r_recv_sem,
):
    nz = n_mp // PAIR
    far = nz // 2
    cols = act.shape[1]
    unit = a_buf.shape[1]
    part = og.shape[0]
    owner = tiles.shape[1]
    nsel = pick.shape[0]
    half = nsel * owner // 2
    dp = lax.axis_index("dp")
    mp = lax.axis_index("mp")
    b = mp // nz
    z = lax.rem(mp, nz)
    right = b * nz + lax.rem(z + 1, nz)
    left = b * nz + lax.rem(z + nz - 1, nz)
    pair = (1 - b) * nz + z
    ways = (right, left)

    def hops(way, u):
        return far if (way + u) % 2 == 0 else far - 1

    def from_z(way, s):
        return s + 1 if way == 0 else nz - 1 - s

    def remote(src, dst, ssem, rsem, where):
        return pltpu.make_async_remote_copy(
            src_ref=src,
            dst_ref=dst,
            send_sem=ssem,
            recv_sem=rsem,
            device_id=where,
            device_id_type=MESH,
        )

    loads = []

    def load(src, dst):
        copy = pltpu.make_async_copy(src, dst, load_sem.at[len(loads)])
        copy.start()
        loads.append(copy)
        return copy

    load_og = load(og, og_buf)
    load_eo = load(eo, eo_buf)
    load_a = [load(act.at[pl.ds(u * unit, unit)], a_buf.at[u, :, pl.ds(0, cols)]) for u in range(UNITS)]

    def k_rows(bb, r):
        return pl.ds(pl.multiple_of((bb * nz + lax.rem(z - r + nz, nz)) * cols, cols), cols)

    load_v = [
        load(vecs.at[k_rows(b, r)], v_buf.at[pl.ds(r * cols, cols), pl.ds(0, cols)]) for r in range(nz)
    ]
    load_q = load(tiles, q_buf)

    barrier = pltpu.get_barrier_semaphore()
    for peer in (right, left, pair):
        pl.semaphore_signal(barrier, inc=1, device_id={"mp": peer}, device_id_type=MESH)
    for o in range(1, n_dp):
        pl.semaphore_signal(
            barrier, inc=1, device_id={"dp": lax.rem(dp + o, n_dp)}, device_id_type=MESH
        )
    pl.semaphore_wait(barrier, 3 + n_dp - 1)

    def a_copy(way, s, u):
        dst = a_buf.at[u, :, pl.ds(from_z(way, s) * cols, cols)]
        if s == 0:
            src = act.at[pl.ds(u * unit, unit)]
        else:
            src = a_buf.at[u, :, pl.ds(from_z(way, s - 1) * cols, cols)]
        return remote(
            src, dst, a_send_sem.at[way, s, u], a_recv_sem.at[way, s, u], {"mp": ways[way]}
        )

    for u in range(UNITS):
        for way in range(2):
            a_copy(way, 0, u).start()

    def v_copy(r):
        return remote(
            vecs.at[k_rows(1 - b, r)],
            v_buf.at[pl.ds(r * cols, cols), pl.ds(cols, cols)],
            v_send_sem.at[r],
            v_recv_sem.at[r],
            {"mp": pair},
        )

    for r in range(nz):
        v_copy(r).start()

    def o_rows(bb, r):
        return pl.ds(pl.multiple_of((bb * nz + lax.rem(z - r + nz, nz)) * part, part), part)

    def o_copy(way, s):
        prev = 0 if s == 0 else from_z(way, s - 1)
        src = ro_buf.at[o_rows(b, prev)]
        return remote(
            src, src, o_send_sem.at[way, s], o_recv_sem.at[way, s], {"mp": ways[way]}
        )

    def ox_copy(r):
        src = ro_buf.at[o_rows(b, r)]
        return remote(src, src, ox_send_sem.at[r], ox_recv_sem.at[r], {"mp": pair})

    def o_arrival(way, s):
        dst = ro_buf.at[o_rows(b, from_z(way, s))]
        return remote(
            dst, dst, o_send_sem.at[way, s], o_recv_sem.at[way, s], {"mp": ways[way]}
        )

    def ox_arrival(r):
        dst = ro_buf.at[o_rows(1 - b, r)]
        return remote(dst, dst, ox_send_sem.at[r], ox_recv_sem.at[r], {"mp": pair})

    load_og.wait()
    load_eo.wait()
    ro_buf[o_rows(b, 0), :] = jnp.dot(
        og_buf[...], eo_buf[...], preferred_element_type=F32
    ).astype(BF16)
    for way in range(2):
        o_copy(way, 0).start()
    ox_copy(0).start()

    for s in range(1, far):
        for u in range(UNITS):
            for way in range(2):
                a_copy(way, s - 1, u).wait_recv()
                if s < hops(way, u):
                    a_copy(way, s, u).start()
        for way in range(2):
            if s - 1 < hops(way, 0):
                o_arrival(way, s - 1).wait_recv()
                if s < hops(way, 0):
                    o_copy(way, s).start()
                ox_copy(from_z(way, s - 1)).start()
    o_arrival(0, far - 1).wait_recv()
    ox_copy(far).start()

    for copy in load_a + load_v + [load_q]:
        copy.wait()
    for r in range(nz):
        v_copy(r).wait_recv()
    for r in range(nz):
        ox_arrival(r).wait_recv()

    def p_copy(u):
        return remote(
            psend.at[u], precv.at[u], p_send_sem.at[u], p_recv_sem.at[u], {"mp": pair}
        )

    def rotate(u):
        a_copy(u % 2, far - 1, u).wait_recv()
        prod = jnp.dot(a_buf[u], v_buf[...], preferred_element_type=F32)
        own_buf[u] = prod[:, :cols]
        psend[u] = prod[:, cols:].astype(BF16)
        p_copy(u).start()

    def document_grads(u):
        p_copy(u).wait_recv()
        rot_t = (own_buf[u] + precv[u].astype(F32)).T.astype(BF16)
        where = slots[:, u * unit : (u + 1) * unit]
        rows = ro_buf[u * unit : (u + 1) * unit, :]

        def one(n, carry):
            mask = (where == n).astype(F32).astype(BF16)
            grad = jnp.dot(rot_t * mask, rows, preferred_element_type=F32)
            if u == 0:
                acc[n] = grad
            elif u < UNITS - 1:
                acc[n] += grad
            else:
                grad += acc[n]
                carry = carry + grad * grad
            return carry

        if u < UNITS - 1:
            lax.fori_loop(0, DOC_G, lambda n, c: (one(n, c), c)[1], 0)
            return None
        total = jnp.zeros(acc.shape[1:], F32)
        for n in range(DOC_G):
            total = one(n, total)
        return total

    for u in range(UNITS):
        rotate(u)
        if u > 0:
            document_grads(u - 1)
    squares = document_grads(UNITS - 1).T
    sq_own[...] = squares.reshape(sq_own.shape)
    sq_send[...] = squares.reshape(sq_send.shape).astype(BF16)

    def sq_copy(o):
        to = lax.rem(dp + o, n_dp)
        return remote(
            sq_send.at[to], sq_recv.at[o - 1], sq_send_sem.at[o - 1], sq_recv_sem.at[o - 1], {"dp": to}
        )

    for o in range(1, n_dp):
        sq_copy(o).start()
    summed = sq_own[dp]
    for o in range(1, n_dp):
        sq_copy(o).wait_recv()
        summed = summed + sq_recv[o - 1].astype(F32)
    damped = summed / (DOC_G * n_dp) + DAMPING
    for s in range(nsel):
        sc[s * owner : (s + 1) * owner, :cols] = (q_buf[pick[s]].astype(F32) / damped).astype(BF16)

    sc_copy = remote(
        sc.at[:, pl.ds(0, cols)], sc.at[:, pl.ds(cols, cols)], sc_sems.at[0], sc_sems.at[1], {"mp": pair}
    )
    sc_copy.start()
    sc_copy.wait_recv()

    def product(r, h):
        return lax.dot_general(
            v_buf[r * cols : (r + 1) * cols, :],
            sc[h * half : (h + 1) * half, :],
            (((1,), (1,)), ((), ())),
            preferred_element_type=F32,
        )

    def r_copy(way, t, h):
        return remote(
            r_send.at[way, h, t],
            r_recv.at[way, h, t],
            r_send_sem.at[way, h, t],
            r_recv_sem.at[way, h, t],
            {"mp": ways[way]},
        )

    for t in range(far):
        for h in range(2):
            for way in range(2):
                reach = hops(way, h)
                if t >= reach:
                    continue
                r = nz - reach + t if way == 0 else reach - t
                mine = product(r, h)
                if t > 0:
                    r_copy(way, t - 1, h).wait_recv()
                    mine = mine + r_recv[way, h, t - 1].astype(F32)
                r_send[way, h, t] = mine.astype(BF16)
                r_copy(way, t, h).start()
    for h in range(2):
        mine = product(0, h)
        for way in range(2):
            last = hops(way, h) - 1
            r_copy(way, last, h).wait_recv()
            mine = mine + r_recv[way, h, last].astype(F32)
        out[:, h * half : (h + 1) * half] = mine.astype(BF16)

    for u in range(UNITS):
        for way in range(2):
            for s in range(hops(way, u)):
                a_copy(way, s, u).wait_send()
        p_copy(u).wait_send()
    for r in range(nz):
        v_copy(r).wait_send()
        ox_copy(r).wait_send()
    for way in range(2):
        for s in range(hops(way, 0)):
            o_copy(way, s).wait_send()
        for h in range(2):
            for t in range(hops(way, h)):
                r_copy(way, t, h).wait_send()
    for o in range(1, n_dp):
        sq_copy(o).wait_send()
    sc_copy.wait_send()


def shards(n_dp, n_mp, act, og, doc_slot, vecs, eo, tiles, pick):
    rows, cols = act.shape
    nz = n_mp // PAIR
    far = nz // 2
    e = eo.shape[0]
    unit = rows // UNITS
    owner = tiles.shape[1]
    nsel = pick.shape[0]
    wide = nsel * owner
    vmem = pl.BlockSpec(memory_space=pltpu.VMEM)
    anywhere = pl.BlockSpec(memory_space=pl.ANY)
    dma = pltpu.SemaphoreType.DMA
    flat = pl.pallas_call(
        functools.partial(fused, n_dp, n_mp),
        out_shape=jax.ShapeDtypeStruct((cols, wide), BF16),
        in_specs=[
            anywhere,
            anywhere,
            vmem,
            anywhere,
            anywhere,
            anywhere,
            pl.BlockSpec(memory_space=pltpu.SMEM),
        ],
        out_specs=vmem,
        scratch_shapes=[
            pltpu.VMEM((UNITS, unit, nz * cols), BF16),
            pltpu.VMEM((nz * cols, 2 * cols), BF16),
            pltpu.VMEM(og.shape, BF16),
            pltpu.VMEM(eo.shape, BF16),
            pltpu.VMEM(tiles.shape, BF16),
            pltpu.VMEM((rows, e), BF16),
            pltpu.VMEM((UNITS, unit, cols), F32),
            pltpu.VMEM((UNITS, unit, cols), BF16),
            pltpu.VMEM((UNITS, unit, cols), BF16),
            pltpu.VMEM((DOC_G, cols, e), F32),
            pltpu.VMEM((n_dp, owner, cols), BF16),
            pltpu.VMEM((n_dp, owner, cols), F32),
            pltpu.VMEM((n_dp - 1, owner, cols), BF16),
            pltpu.VMEM((wide, 2 * cols), BF16),
            pltpu.VMEM((2, 2, far, cols, wide // 2), BF16),
            pltpu.VMEM((2, 2, far, cols, wide // 2), BF16),
            dma((3 + UNITS + nz,)),
            dma((2, far, UNITS)),
            dma((2, far, UNITS)),
            dma((nz,)),
            dma((nz,)),
            dma((2, far)),
            dma((2, far)),
            dma((nz,)),
            dma((nz,)),
            dma((UNITS,)),
            dma((UNITS,)),
            dma((n_dp - 1,)),
            dma((n_dp - 1,)),
            dma((2,)),
            dma((2, 2, far)),
            dma((2, 2, far)),
        ],
        compiler_params=pltpu.CompilerParams(
            collective_id=0, has_side_effects=True, vmem_limit_bytes=48 * 1024 * 1024
        ),
        cost_estimate=pl.CostEstimate(
            flops=6_000_000_000, bytes_accessed=8_000_000, transcendentals=0
        ),
    )(act, og, doc_slot.reshape(1, rows), vecs, eo, tiles, pick)
    return flat.reshape(cols, nsel, owner)


def solution(mesh):
    in_specs = (
        P("dp", "mp"),
        P(("dp", "mp"), None),
        P("dp"),
        P(None, "mp"),
        P(),
        P(None, "dp", "mp"),
        P(),
    )
    out_specs = P("mp", None, "dp")
    body = functools.partial(shards, mesh.shape["dp"], mesh.shape["mp"])
    return jax.shard_map(body, mesh=mesh, in_specs=in_specs, out_specs=out_specs, check_vma=False)
```

time: 478 us -> 124 us (0.26)
  waiting for transfers between devices: 438 us -> 0 us
  Pallas kernels: 0 us -> 116 us
  matrix products: 21 us -> 0 us
  between operations: 13.2 us -> 0.02 us
  local copies, waits for them, and re-layouts: 0.74 us -> 7.74 us
    all_gather x2 -> x0, waiting for transfers between devices: 193 us -> none  [the longest x1 121 us: shards(): lax.all_gather(activations, 'mp', axis=1, tiled=True)]
    psum x1 -> x0, waiting for transfers between devices: 142 us -> none  [shards(): summed = lax.psum(partial_sq, 'dp')]
    pallas_call x0 -> x1, Pallas kernels: none -> 116 us  [shards(): pl.pallas_call(functools.partial(fused, n_dp, n_mp), out_shape=jax.ShapeD...]
    reduce_scatter x1 -> x0, waiting for transfers between devices: 102 us -> none  [shards(): lax.psum_scatter(lax.dot_general(basis_part, flat_tiles, (((1,), (1,)), (...]
    dot_general x3 -> x0, matrix products: 21 us -> none  [the longest x1 13.3 us: shards(): jnp.einsum('nre,rk->nek', masked_entries, rotated_in, preferred_element_t...]
    unnamed x6 -> x14, local copies, waits for them, and re-layouts: 0.01 us -> 6.89 us
  transfers between devices with their start and end apart: 4 -> 0, of which waited for: 4 -> 0; matrix products, arithmetic and copies ran while one was open for 1% -> 0% of each run, Pallas kernels for 0% -> 0%
where the time goes in v1:
time: 124 us
  Pallas kernels  116 us (94%)
  local copies, waits for them, and re-layouts  7.74 us (6%)
    pallas_call x1, Pallas kernels, shards(): pl.pallas_call(functools.partial(fused, n_dp, n_mp), out_shape=jax.ShapeD...  116 us
    unnamed x14, local copies, waits for them, and re-layouts  6.89 us

profile of v1, /device:TPU:2, one launch (start us, length us, event | category | flops | bytes accessed | tf_op | source)
XLA Modules:
  0.0 123.6 jit_solution(11932617048730300819)
XLA Ops:
  0.0 0.0 copy-start
  0.0 1.6 %copy-done = bf16[4096,256]{1,0:T(8,128)(2,1)S(1)} copy-done((bf16[4096,256]{1,0:T(8,128)(2,1)S(1)}, bf16[4096,256]{1,0:T(8,128)(2,1)}, u32[]{:S(2)}) %copy-start) | copy-done | bytes 2097176
  1.6 0.0 copy-start.1
  1.6 1.0 copy-done.1
  2.6 0.0 copy-start.2
  2.6 1.0 copy-done.2
  3.7 0.0 copy-start.3
  3.7 1.0 copy-done.3
  4.7 0.0 copy-start.4
  4.7 0.8 copy-done.4
  5.6 0.0 copy-start.5
  5.6 0.7 copy-done.5
  6.2 0.0 copy-start.6
  6.2 0.7 copy-done.6
  6.9 115.8 %shard_map.73 = bf16[256,512]{1,0:T(8,128)(2,1)S(1)} custom-call(bf16[1024,256]{1,0:T(8,128)(2,1)S(1)} %copy-done.1, bf16[64,512]{1,0:T(8,128)(2,1)S(1)} %copy-done.4, s32[1,1024]{1,0:T(1,128)S(1)} %bitcast.2, bf16[4096,256]{1,0:T(8,128)(2,1)S(1)} %copy-done, bf16[512,512]{1,0:T(8,128)(2,1)S(1)} %copy-done.2, bf16[32,32,256]{2,1,0:T(8,128)(2,1)S(1)} %copy-done.3, ...), custom_call_target="tpu_custom_call" | custom-call | flops 6000000000 | bytes 8000000 | tf_op jit(solution)/shard_map/pallas_call | solution.py:343
  122.7 0.8 copy.9
Async XLA Ops:
  0.0 1.6 %copy-start = (bf16[4096,256]{1,0:T(8,128)(2,1)S(1)}, bf16[4096,256]{1,0:T(8,128)(2,1)}, u32[]{:S(2)}) copy-start(bf16[4096,256]{1,0:T(8,128)(2,1)} %vecs.1) | copy-start | bytes 6291460
  1.6 1.0 copy-start.1
  2.6 1.0 copy-start.2
  3.7 1.0 copy-start.3
  4.7 0.8 copy-start.4
  5.6 0.7 copy-start.5
  6.2 0.7 copy-start.6
